TPU v7x, 32 devices: a whole 2x2x4 slice. The times are simulated.
32 devices in a mesh: ctx: 4 (over x, core), ch: 8 (over z, y).
Axes of the slice: x: 2, y: 2, z: 4, core: 2. Of those that a mesh axis runs over, the one named last changes fastest.
Arguments:
- value_in: bfloat16 [8192, 2048], P('ch', 'ctx'), may hold values from -6 to 6
- key_in: bfloat16 [8192, 2048], P('ch', 'ctx'), may hold values from -6 to 6
- gate_first: bfloat16 [8192, 2048], P('ch', 'ctx'), may hold values from -6 to 6
- gate_second: bfloat16 [8192, 2048], P('ch', 'ctx'), may hold values from -6 to 6
- gate_long: bfloat16 [8192, 2048], P('ch', 'ctx'), may hold values from -6 to 6
- filter_first: bfloat16 [512, 128], P('ch'), may hold values from -0.5 to 0.5
- filter_second: bfloat16 [512, 128], P('ch'), may hold values from -0.5 to 0.5
- long_filter: bfloat16 [8192, 2048], P(('ch', 'ctx')), may hold values from -0.125 to 0.125
- skip_gain: float32 [8192], P('ch'), may hold values from 0.5 to 1.5
Outputs:
- mixed_out: bfloat16 [8192, 2048], P('ch', 'ctx')
All inputs are finite; a program needn't handle non-finite values.
Results may differ from a plain program's by a relative error of at most 0.0085.
Values may be sent and summed in bfloat16 or wider, within the bound.
A program may use at most 64 MiB of HBM per device.

v0:
```python
import cmath
import functools
import math

import jax
import jax.numpy as jnp
import ml_dtypes
import numpy as np
from jax import lax
from jax.experimental import pallas as pl
from jax.experimental.pallas import tpu as pltpu
from jax.sharding import PartitionSpec as P

HIGH = lax.Precision.HIGH
LANES = 128
ROWS = 16
MESH = pl.DeviceIdType.MESH


def from_behind(shard, axis, by):
    devices = lax.axis_size(axis)
    pairs = [(i, i + by) for i in range(devices) if 0 <= i + by < devices]
    return lax.ppermute(shard, axis, pairs)


def band_matrix(filters, tap_count):
    group_count = filters.shape[0]
    zero_one = jnp.zeros((group_count, 1), filters.dtype)
    zero_rest = jnp.zeros((group_count, tap_count), filters.dtype)
    pattern = jnp.concatenate([zero_one, jnp.flip(filters, axis=1), zero_rest], axis=1)
    tiled = jnp.tile(pattern, (1, tap_count))
    return tiled[:, : tap_count * 2 * tap_count].reshape(group_count, tap_count, 2 * tap_count)


def toeplitz_conv(extended, filters, tap_count):
    channels, total_len = extended.shape
    length = total_len - tap_count
    block_count = length // tap_count
    front_half = extended[:, :length].reshape(channels, block_count, tap_count)
    back_half = extended[:, tap_count:].reshape(channels, block_count, tap_count)
    windows = jnp.concatenate([front_half, back_half], axis=2)
    group_count = filters.shape[0]
    windows = windows.reshape(group_count, channels // group_count, block_count, 2 * tap_count)
    toeplitz = band_matrix(filters, tap_count)
    result = jnp.einsum("gts,gcbs->gcbt", toeplitz, windows, preferred_element_type=jnp.float32)
    return result.reshape(channels, length)


def previous_rim(tail):
    return from_behind(tail, "ctx", 1)


def to_channels(data):
    return lax.all_to_all(data, "ctx", split_axis=0, concat_axis=1, tiled=True)


def first_section(mixed_in, gate_first, filter_first, tap_count):
    length = mixed_in.shape[1]
    extended = jnp.concatenate([previous_rim(mixed_in[:, length - tap_count :]), mixed_in], axis=1)
    return (
        gate_first.astype(jnp.float32) * toeplitz_conv(extended, filter_first, tap_count)
    ).astype(jnp.bfloat16)


def dft_tables(size):
    index = jnp.arange(size, dtype=jnp.int32)
    angle = (index[:, None] * index[None, :] % size).astype(jnp.float32) * (-2.0 * math.pi / size)
    return (jnp.cos(angle), jnp.sin(angle))


def split_factor(padded_len):
    outer = 2
    cand = 2
    while cand * cand <= padded_len:
        if padded_len % cand == 0:
            outer = cand
        cand = cand + 2
    return outer


def long_convolution(signal, filt_vals, skip_part):
    channels, length = signal.shape
    padded_len = 2 * length
    rows_outer = split_factor(padded_len)
    rows_inner = padded_len // rows_outer
    half_rows = rows_outer // 2
    outer_cos, outer_sin = dft_tables(rows_outer)
    inner_cos, inner_sin = dft_tables(rows_inner)
    k_index = jnp.arange(rows_outer, dtype=jnp.int32)[:, None]
    n_index = jnp.arange(rows_inner, dtype=jnp.int32)[None, :]
    twid_angle = (k_index * n_index % padded_len).astype(jnp.float32) * (
        -2.0 * math.pi / padded_len
    )
    twid_cos = jnp.cos(twid_angle)
    twid_sin = jnp.sin(twid_angle)
    outer_table = jnp.concatenate([outer_cos[:, :half_rows], outer_sin[:, :half_rows]], axis=0)
    inner_fwd = jnp.concatenate(
        [
            jnp.concatenate([inner_cos, inner_sin], axis=1),
            jnp.concatenate([-inner_sin, inner_cos], axis=1),
        ],
        axis=0,
    )
    inner_back = jnp.concatenate(
        [
            jnp.concatenate([inner_cos, -inner_sin], axis=1),
            jnp.concatenate([inner_sin, inner_cos], axis=1),
        ],
        axis=0,
    )

    def forward(values):
        grid = values.reshape(channels, half_rows, rows_inner)
        parts = jnp.einsum("kn,cnm->ckm", outer_table, grid, precision=HIGH)
        part_re = parts[:, :rows_outer]
        part_im = parts[:, rows_outer:]
        turned_re = part_re * twid_cos - part_im * twid_sin
        turned_im = part_re * twid_sin + part_im * twid_cos
        turned = jnp.concatenate([turned_re, turned_im], axis=2)
        spectrum = jnp.einsum("ckn,nm->ckm", turned, inner_fwd, precision=HIGH)
        return (spectrum[:, :, :rows_inner], spectrum[:, :, rows_inner:])

    sig_re, sig_im = forward(signal)
    filt_re, filt_im = forward(filt_vals)
    prod_re = sig_re * filt_re - sig_im * filt_im
    prod_im = sig_re * filt_im + sig_im * filt_re
    stacked = jnp.concatenate([prod_re, prod_im], axis=2)
    back = jnp.einsum("ckm,mn->ckn", stacked, inner_back, precision=HIGH)
    back_re = back[:, :, :rows_inner]
    back_im = back[:, :, rows_inner:]
    reverted_re = back_re * twid_cos + back_im * twid_sin
    reverted_im = back_im * twid_cos - back_re * twid_sin
    reverted = jnp.concatenate([reverted_re, reverted_im], axis=1)
    result = jnp.einsum("kn,ckm->cnm", outer_table, reverted, precision=HIGH)
    result = result.reshape(channels, length) / padded_len
    return skip_part[:, None] * signal + result


def shards_general(
    value_in,
    key_in,
    gate_first,
    gate_second,
    gate_long,
    filter_first,
    filter_second,
    long_filter,
    skip_gain,
):
    tap_count = filter_first.shape[1]
    channels, length = value_in.shape
    per_device = channels // lax.axis_size("ctx")
    channel_base = lax.axis_index("ctx") * per_device
    mixed_in = (key_in.astype(jnp.float32) * value_in.astype(jnp.float32)).astype(jnp.bfloat16)
    first_out = first_section(mixed_in, gate_first, filter_first, tap_count)
    prior_first = from_behind(first_out[:, length - tap_count :], "ctx", 1)
    first_wide = jnp.concatenate([prior_first, first_out], axis=1)
    second_out = (
        gate_second.astype(jnp.float32) * toeplitz_conv(first_wide, filter_second, tap_count)
    ).astype(jnp.bfloat16)
    moved = to_channels(second_out)
    skip_here = lax.dynamic_slice_in_dim(skip_gain, channel_base, per_device, 0)
    filt_vals = long_filter.astype(jnp.float32)
    long_out = long_convolution(moved.astype(jnp.float32), filt_vals, skip_here).astype(
        jnp.bfloat16
    )
    back_home = lax.all_to_all(long_out, "ctx", split_axis=1, concat_axis=0, tiled=True)
    return (gate_long.astype(jnp.float32) * back_home.astype(jnp.float32)).astype(jnp.bfloat16)


def unit(numerator, denominator):
    return cmath.exp(-2j * math.pi * numerator / denominator)


def turn(value, factor):
    re, im = value
    if abs(factor - 1) < 1e-12:
        return value
    if abs(factor + 1j) < 1e-12:
        return (im, -re)
    if abs(factor - 1j) < 1e-12:
        return (-im, re)
    if abs(abs(factor.real) - abs(factor.imag)) < 1e-12:
        size = abs(factor.real)
        re, im = re * size, im * size
        if factor.real > 0 and factor.imag < 0:
            return (re + im, im - re)
        if factor.real < 0 and factor.imag < 0:
            return (im - re, -re - im)
        if factor.real > 0:
            return (re - im, re + im)
        return (-re - im, re - im)
    return (re * factor.real - im * factor.imag, re * factor.imag + im * factor.real)


def complex_dft(values, sign):
    count = len(values)
    if count == 1:
        return values
    half = count // 2
    low, high = [], []
    for a in range(half):
        (p_re, p_im), (q_re, q_im) = values[a], values[a + half]
        low.append((p_re + q_re, p_im + q_im))
        factor = unit(a, count)
        high.append(turn((p_re - q_re, p_im - q_im), factor if sign > 0 else factor.conjugate()))
    result = [None] * count
    result[0::2] = complex_dft(low, sign)
    result[1::2] = complex_dft(high, sign)
    return result


def odd_bins(values):
    count = len(values)
    if count == 1:
        return {1: (values[0], None)}
    half = count // 2
    folded = [turn((values[a], -values[a + half]), unit(a, 2 * count)) for a in range(half)]
    bins = {}
    for place, (re, im) in enumerate(complex_dft(folded, 1)):
        r = 4 * place + 1
        if r < count:
            bins[r] = (re, im)
        else:
            bins[2 * count - r] = (re, -im)
    return bins


def real_bins(values):
    count = len(values)
    if count == 1:
        return {0: (values[0], None)}
    half = count // 2
    even = real_bins([values[a] + values[a + half] for a in range(half)])
    odd = odd_bins([values[a] - values[a + half] for a in range(half)])
    bins = {2 * r: v for r, v in even.items()}
    bins.update(odd)
    return bins


def padded_bins(values):
    bins = {2 * r: v for r, v in real_bins(values).items()}
    bins.update(odd_bins(values))
    return bins


def odd_back(bins, count):
    if count == 1:
        return [bins[1][0]]
    half = count // 2
    folded = []
    for place in range(half):
        r = 4 * place + 1
        if r < count:
            folded.append(bins[r])
        else:
            re, im = bins[2 * count - r]
            folded.append((re, -im))
    spread = complex_dft(folded, -1)
    spread = [turn(spread[a], unit(a, 2 * count).conjugate()) for a in range(half)]
    return [v[0] for v in spread] + [-v[1] for v in spread]


def real_back(bins, count):
    if count == 1:
        return [bins[0][0]]
    half = count // 2
    even = real_back({r // 2: v for r, v in bins.items() if r % 2 == 0}, half)
    odd = odd_back({r: v for r, v in bins.items() if r % 2 == 1}, half)
    return [even[a] + odd[a] for a in range(half)] + [even[a] - odd[a] for a in range(half)]


def padded_back(bins, count):
    even = real_back({r // 2: v for r, v in bins.items() if r % 2 == 0}, count)
    odd = odd_back({r: v for r, v in bins.items() if r % 2 == 1}, count)
    return [even[a] + odd[a] for a in range(count)]


def inner_tables(length):
    padded_len = 2 * length
    outer = padded_len // LANES
    b = np.arange(LANES)[:, None]
    q = np.arange(LANES)[None, :]
    forward, back = [], []
    for r in range(outer // 2 + 1):
        angle = (b * (r + outer * q) % padded_len) * (-2.0 * math.pi / padded_len)
        c, s = np.cos(angle), np.sin(angle)
        table = np.block([[c, s], [-s, c]])
        weight = (1.0 if r in (0, outer // 2) else 2.0) / padded_len
        forward.append(table)
        back.append(table.T * weight)
    return (
        np.stack(forward).astype(ml_dtypes.bfloat16),
        np.stack(back).astype(ml_dtypes.bfloat16),
    )


def band(row):
    rolled = pltpu.roll(jnp.broadcast_to(row, (LANES, LANES)), 0, 1, stride=1, stride_axis=0)
    s = lax.broadcasted_iota(jnp.int32, (LANES, LANES), 0)
    t = lax.broadcasted_iota(jnp.int32, (LANES, LANES), 1)
    zero = jnp.zeros((LANES, LANES), jnp.float32)
    return jnp.concatenate(
        [jnp.where(t < s, rolled, zero), jnp.where(t >= s, rolled, zero)], axis=0
    ).astype(jnp.bfloat16)


def gated(gate, value):
    return (gate.astype(jnp.float32) * value).astype(jnp.bfloat16)


def whole_kernel(
    n,
    chunk,
    value_ref,
    key_ref,
    gate_first_ref,
    filter_first_ref,
    filter_second_ref,
    skip_ref,
    gate_second_hbm,
    gate_long_hbm,
    long_filter_hbm,
    forward_hbm,
    back_hbm,
    out_ref,
    gate_second,
    gate_long,
    long_filter,
    forward,
    backward,
    taps_first,
    taps_second,
    band_first,
    band_second,
    mixed,
    first,
    halo_mixed,
    halo_first,
    second,
    gathered,
    long_out,
    returned,
    skip_wide,
    bins_in,
    spectrum,
    bins_out,
    load_sem,
    rim_send,
    rim_recv,
    there_send,
    there_recv,
    home_send,
    home_recv,
):
    _, per, length = value_ref.shape
    me = lax.axis_index("ctx")
    blocks = length // LANES
    chunks = per // chunk
    groups = chunk // ROWS
    total_blocks = n * blocks
    bin_count = total_blocks + 1
    last = slice(length - LANES, length)

    barrier = pltpu.get_barrier_semaphore()
    for k in range(1, n):
        pl.semaphore_signal(
            barrier, inc=1, device_id={"ctx": lax.rem(me + k, n)}, device_id_type=MESH
        )

    loads = [
        pltpu.make_async_copy(src, dst, load_sem.at[i])
        for i, (src, dst) in enumerate(
            [
                (gate_second_hbm, gate_second),
                (long_filter_hbm, long_filter),
                (forward_hbm, forward),
                (back_hbm, backward),
                (gate_long_hbm, gate_long),
            ]
        )
    ]
    for load in loads:
        load.start()

    def part(q):
        return pl.ds(pl.multiple_of(q * chunk, chunk), chunk)

    def rim(which, q):
        src, dst = ((mixed, halo_mixed), (first, halo_first))[which]
        return pltpu.make_async_remote_copy(
            src_ref=src.at[:, part(q), last],
            dst_ref=dst.at[:, part(q), :],
            send_sem=rim_send.at[which, q],
            recv_sem=rim_recv.at[which, q],
            device_id={"ctx": lax.rem(me + 1, n)},
            device_id_type=MESH,
        )

    def there(k, q, arriving=False):
        peer = lax.rem(me + (n - k if arriving else k), n)
        slot = peer if arriving else me
        return pltpu.make_async_remote_copy(
            src_ref=second.at[peer, part(q), :],
            dst_ref=gathered.at[slot, part(q), :],
            send_sem=there_send.at[k, q],
            recv_sem=there_recv.at[k, q],
            device_id={"ctx": peer},
            device_id_type=MESH,
        )

    def home(k, q, arriving=False):
        peer = lax.rem(me + (n - k if arriving else k), n)
        slot = peer if arriving else me
        return pltpu.make_async_remote_copy(
            src_ref=long_out.at[peer, part(q), :],
            dst_ref=returned.at[slot, part(q), :],
            send_sem=home_send.at[k, q],
            recv_sem=home_recv.at[k, q],
            device_id={"ctx": peer},
            device_id_type=MESH,
        )

    def rows_at(q, j):
        return pl.ds(pl.multiple_of(q * chunk + j * ROWS, ROWS), ROWS)

    def lanes(b):
        return slice(b * LANES, (b + 1) * LANES)

    taps_first[...] = filter_first_ref[...].astype(jnp.float32)
    taps_second[...] = filter_second_ref[...].astype(jnp.float32)
    eye = lax.broadcasted_iota(jnp.int32, (LANES, LANES), 0) == lax.broadcasted_iota(
        jnp.int32, (LANES, LANES), 1
    )
    for i in range(per // LANES):
        line = skip_ref[pl.ds(me * (per // LANES) + i, 1), :]
        column = jnp.sum(jnp.where(eye, line, 0.0), axis=1, keepdims=True)
        skip_wide[i * LANES : (i + 1) * LANES, :] = jnp.broadcast_to(column, (LANES, LANES))

    pl.semaphore_wait(barrier, n - 1)

    @pl.when(me == 0)
    def _():
        halo_mixed[...] = jnp.zeros_like(halo_mixed)
        halo_first[...] = jnp.zeros_like(halo_first)

    def early(q, _):
        def multiply(d, _):
            mixed[d, part(q), :] = (
                key_ref[d, part(q), :].astype(jnp.float32)
                * value_ref[d, part(q), :].astype(jnp.float32)
            ).astype(jnp.bfloat16)
            return 0

        lax.fori_loop(0, n, multiply, 0)

        @pl.when(me < n - 1)
        def _():
            rim(0, q).start()

        def one(d, _):
            for j in range(groups):
                g = d * (per // ROWS) + q * groups + j
                w = band(taps_first[pl.ds(g, 1), :])
                band_first[g] = w
                band_second[g] = band(taps_second[pl.ds(g, 1), :])
                rows = rows_at(q, j)
                windows = jnp.concatenate(
                    [mixed[d, rows, b * LANES - LANES : (b + 1) * LANES] for b in range(1, blocks)],
                    axis=0,
                )
                result = jnp.dot(windows, w, preferred_element_type=jnp.float32)
                for b in range(1, blocks):
                    first[d, rows, lanes(b)] = gated(
                        gate_first_ref[d, rows, lanes(b)], result[(b - 1) * ROWS : b * ROWS]
                    )
            return 0

        lax.fori_loop(0, n, one, 0)

        @pl.when(me < n - 1)
        def _():
            rim(1, q).start()

        return 0

    lax.fori_loop(0, chunks, early, 0)
    loads[0].wait()

    def late(q, _):
        @pl.when(me > 0)
        def _():
            rim(0, q).wait_recv()
            rim(1, q).wait_recv()

        for k in [*range(2, n), 1, 0]:
            d = lax.rem(me + k, n)
            target = second if k else gathered
            for j in range(groups):
                g = d * (per // ROWS) + q * groups + j
                rows = rows_at(q, j)
                head = jnp.concatenate([halo_mixed[d, rows, :], mixed[d, rows, lanes(0)]], axis=1)
                head = jnp.dot(head, band_first[g], preferred_element_type=jnp.float32)
                head = gated(gate_first_ref[d, rows, lanes(0)], head)
                parts = [halo_first[d, rows, :], head]
                parts += [first[d, rows, lanes(b)] for b in range(1, blocks)]
                windows = jnp.concatenate(
                    [
                        jnp.concatenate([parts[b], parts[b + 1]], axis=1)
                        for b in range(blocks)
                    ],
                    axis=0,
                )
                result = jnp.dot(windows, band_second[g], preferred_element_type=jnp.float32)
                for b in range(blocks):
                    target[d, rows, lanes(b)] = gated(
                        gate_second[d, rows, lanes(b)], result[b * ROWS : (b + 1) * ROWS]
                    )
            if k:
                there(k, q).start()
        return 0

    lax.fori_loop(0, chunks, late, 0)

    def spread(values, at):
        bins = padded_bins(values)
        for r in range(bin_count):
            re, im = bins[r]
            im = jnp.zeros_like(re) if im is None else im
            bins_in[r, at, :] = jnp.concatenate([re, im], axis=1).astype(jnp.bfloat16)

    loads[1].wait()
    loads[2].wait()

    def filter_rows(j, _):
        at = pl.ds(pl.multiple_of(j * ROWS, ROWS), ROWS)
        spread([long_filter[at, lanes(a)].astype(jnp.float32) for a in range(total_blocks)], at)
        return 0

    lax.fori_loop(0, per // ROWS, filter_rows, 0)

    def filter_bin(r, _):
        spectrum[r] = jnp.dot(bins_in[r], forward[r], preferred_element_type=jnp.float32)
        return 0

    lax.fori_loop(0, bin_count, filter_bin, 0)
    loads[3].wait()

    def convolve(q, _):
        for k in range(1, n):
            there(k, q, True).wait_recv()

        def signal(j, rows):
            return [
                gathered[a // blocks, rows, lanes(a % blocks)].astype(jnp.float32)
                for a in range(total_blocks)
            ]

        def rows_in(j, _):
            at = pl.ds(pl.multiple_of(j * ROWS, ROWS), ROWS)
            spread(signal(j, rows_at(q, j)), at)
            return 0

        lax.fori_loop(0, groups, rows_in, 0)

        for r in range(bin_count):
            sig = jnp.dot(bins_in[r, 0:chunk, :], forward[r], preferred_element_type=jnp.float32)
            filt = spectrum[r, part(q), :]
            sig_re, sig_im = sig[:, :LANES], sig[:, LANES:]
            filt_re, filt_im = filt[:, :LANES], filt[:, LANES:]
            product = jnp.concatenate(
                [sig_re * filt_re - sig_im * filt_im, sig_re * filt_im + sig_im * filt_re], axis=1
            ).astype(jnp.bfloat16)
            bins_out[r] = jnp.dot(product, backward[r], preferred_element_type=jnp.float32)

        def rows_out(j, _):
            at = pl.ds(pl.multiple_of(j * ROWS, ROWS), ROWS)
            rows = rows_at(q, j)
            bins = {
                r: (bins_out[r, at, :LANES], bins_out[r, at, LANES:]) for r in range(bin_count)
            }
            result = padded_back(bins, total_blocks)
            skip = skip_wide[rows, :]
            for a, value in enumerate(signal(j, rows)):
                long_out[a // blocks, rows, lanes(a % blocks)] = (
                    skip * value + result[a]
                ).astype(jnp.bfloat16)
            return 0

        lax.fori_loop(0, groups, rows_out, 0)
        for k in range(1, n):
            home(k, q).start()
        returned[me, part(q), :] = long_out[me, part(q), :]
        return 0

    lax.fori_loop(0, chunks, convolve, 0)
    loads[4].wait()

    def finish(q, _):
        for k in range(n):
            if k:
                home(k, q, True).wait_recv()
            p = lax.rem(me + (n - k), n)
            out_ref[p, part(q), :] = gated(
                gate_long[p, part(q), :], returned[p, part(q), :].astype(jnp.float32)
            )
        return 0

    lax.fori_loop(0, chunks, finish, 0)

    def drain(q, _):
        @pl.when(me < n - 1)
        def _():
            rim(0, q).wait_send()
            rim(1, q).wait_send()

        for k in range(1, n):
            there(k, q).wait_send()
            home(k, q).wait_send()
        return 0

    lax.fori_loop(0, chunks, drain, 0)


def fits_kernel(channels, length, n, tap_count):
    per = channels // n
    total = n * length
    return (
        tap_count == LANES
        and length % LANES == 0
        and length >= 2 * LANES
        and per % LANES == 0
        and n > 1
        and total & (total - 1) == 0
        and total <= 2048
        and channels * total <= 1024 * 2048
    )


def shards(
    value_in,
    key_in,
    gate_first,
    gate_second,
    gate_long,
    filter_first,
    filter_second,
    long_filter,
    skip_gain,
):
    channels, length = value_in.shape
    n = lax.axis_size("ctx")
    if not fits_kernel(channels, length, n, filter_first.shape[1]):
        return shards_general(
            value_in,
            key_in,
            gate_first,
            gate_second,
            gate_long,
            filter_first,
            filter_second,
            long_filter,
            skip_gain,
        )
    per = channels // n
    total = n * length
    chunk = 64
    chunks = per // chunk
    group_count = filter_first.shape[0]
    bin_count = total // LANES + 1
    cut = lambda a: a.reshape(n, per, length)
    forward, back = inner_tables(total)
    bf16, f32 = jnp.bfloat16, jnp.float32
    vmem = pl.BlockSpec(memory_space=pltpu.VMEM)
    anywhere = pl.BlockSpec(memory_space=pl.ANY)
    dma = pltpu.SemaphoreType.DMA
    out = pl.pallas_call(
        functools.partial(whole_kernel, n, chunk),
        out_shape=jax.ShapeDtypeStruct((n, per, length), bf16),
        in_specs=[vmem] * 6 + [anywhere] * 5,
        out_specs=vmem,
        scratch_shapes=[
            pltpu.VMEM((n, per, length), bf16),
            pltpu.VMEM((n, per, length), bf16),
            pltpu.VMEM((per, total), bf16),
            pltpu.VMEM(forward.shape, bf16),
            pltpu.VMEM(back.shape, bf16),
            pltpu.VMEM(filter_first.shape, f32),
            pltpu.VMEM(filter_second.shape, f32),
            pltpu.VMEM((group_count, 2 * LANES, LANES), bf16),
            pltpu.VMEM((group_count, 2 * LANES, LANES), bf16),
            pltpu.VMEM((n, per, length), bf16),
            pltpu.VMEM((n, per, length), bf16),
            pltpu.VMEM((n, per, LANES), bf16),
            pltpu.VMEM((n, per, LANES), bf16),
            pltpu.VMEM((n, per, length), bf16),
            pltpu.VMEM((n, per, length), bf16),
            pltpu.VMEM((n, per, length), bf16),
            pltpu.VMEM((n, per, length), bf16),
            pltpu.VMEM((per, LANES), f32),
            pltpu.VMEM((bin_count, per, 2 * LANES), bf16),
            pltpu.VMEM((bin_count, per, 2 * LANES), f32),
            pltpu.VMEM((bin_count, chunk, 2 * LANES), f32),
            dma((5,)),
            dma((2, chunks)),
            dma((2, chunks)),
            dma((n, chunks)),
            dma((n, chunks)),
            dma((n, chunks)),
            dma((n, chunks)),
        ],
        compiler_params=pltpu.CompilerParams(
            collective_id=0, has_side_effects=True, vmem_limit_bytes=56 * 1024 * 1024
        ),
        cost_estimate=pl.CostEstimate(
            flops=8 * channels * length * 2 * LANES + 6 * 2 * per * total * 2 * LANES * 2,
            bytes_accessed=8 * channels * length * 2,
            transcendentals=0,
        ),
    )(
        cut(value_in),
        cut(key_in),
        cut(gate_first),
        filter_first,
        filter_second,
        skip_gain.reshape(channels // LANES, LANES),
        cut(gate_second),
        cut(gate_long),
        long_filter,
        jnp.asarray(forward),
        jnp.asarray(back),
    )
    return out.reshape(channels, length)


def solution(mesh):
    placed = (
        P("ch", "ctx"),
        P("ch", "ctx"),
        P("ch", "ctx"),
        P("ch", "ctx"),
        P("ch", "ctx"),
        P("ch", None),
        P("ch", None),
        P(("ch", "ctx"), None),
        P("ch"),
    )
    return jax.shard_map(
        shards, mesh=mesh, in_specs=placed, out_specs=P("ch", "ctx"), check_vma=False
    )
```

profile of v0, /device:TPU:1, one launch (start us, length us, event | category | flops | bytes accessed | tf_op | source)
XLA Modules:
  0.0 37.6 jit_solution(9027440259705790776)
XLA Ops:
  0.0 35.3 %shard_map.109 = bf16[4,256,512]{2,1,0:T(8,128)(2,1)} custom-call(bf16[4,256,512]{2,1,0:T(8,128)(2,1)} %bitcast.8, bf16[4,256,512]{2,1,0:T(8,128)(2,1)} %bitcast.9, bf16[4,256,512]{2,1,0:T(8,128)(2,1)} %bitcast.10, bf16[64,128]{1,0:T(8,128)(2,1)} %filter_first_ref.1, bf16[64,128]{1,0:T(8,128)(2,1)} %filter_second_ref.1, f32[8,128]{1,0:T(8,128)} %bitcast.13, ...), custom_call_target="tpu_custom_call" | custom-call | flops 4294967296 | bytes 8388608 | tf_op jit(solution)/shard_map/pallas_call | solution.py:677
  35.3 2.3 %copy.13 = bf16[1024,512]{1,0:T(8,128)(2,1)} copy(bf16[1024,512]{1,0:T(8,128)(2,1)} %bitcast.7) | data formatting | bytes 2097152
where the time goes:
time: 37.7 us; the launch traced here: 37.6 us
  Pallas kernels  35.3 us (94%)
  local copies, waits for them, and re-layouts  2.26 us (6%)
    pallas_call x1, Pallas kernels, shards(): pl.pallas_call(functools.partial(whole_kernel, n, chunk), out_shape=jax.S...  35.3 us
    unnamed x1, local copies, waits for them, and re-layouts  2.26 us

commit v1 on v0

--- a/solution.py
+++ b/solution.py
@@ -312,20 +312,21 @@
 def whole_kernel(
     n,
     chunk,
+    filter_first_ref,
+    filter_second_ref,
+    skip_ref,
+    value_hbm,
+    key_hbm,
+    gate_first_hbm,
+    gate_second_hbm,
+    long_filter_hbm,
+    forward_hbm,
+    back_hbm,
+    returned,
     value_ref,
     key_ref,
     gate_first_ref,
-    filter_first_ref,
-    filter_second_ref,
-    skip_ref,
-    gate_second_hbm,
-    gate_long_hbm,
-    long_filter_hbm,
-    forward_hbm,
-    back_hbm,
-    out_ref,
     gate_second,
-    gate_long,
     long_filter,
     forward,
     backward,
@@ -340,12 +341,13 @@
     second,
     gathered,
     long_out,
-    returned,
     skip_wide,
     bins_in,
     spectrum,
     bins_out,
     load_sem,
+    part_sem,
+    own_sem,
     rim_send,
     rim_recv,
     there_send,
@@ -353,7 +355,7 @@
     home_send,
     home_recv,
 ):
-    _, per, length = value_ref.shape
+    _, per, length = value_hbm.shape
     me = lax.axis_index("ctx")
     blocks = length // LANES
     chunks = per // chunk
@@ -368,23 +370,36 @@
             barrier, inc=1, device_id={"ctx": lax.rem(me + k, n)}, device_id_type=MESH
         )
 
+    def part(q):
+        return pl.ds(pl.multiple_of(q * chunk, chunk), chunk)
+
+    def loaded(i, q):
+        src, dst = (
+            (key_hbm, key_ref),
+            (value_hbm, value_ref),
+            (gate_first_hbm, gate_first_ref),
+            (gate_second_hbm, gate_second),
+        )[i]
+        return pltpu.make_async_copy(
+            src.at[:, part(q), :], dst.at[:, part(q), :], part_sem.at[i, q]
+        )
+
+    for q in range(chunks):
+        for i in range(4):
+            loaded(i, q).start()
     loads = [
         pltpu.make_async_copy(src, dst, load_sem.at[i])
         for i, (src, dst) in enumerate(
-            [
-                (gate_second_hbm, gate_second),
-                (long_filter_hbm, long_filter),
-                (forward_hbm, forward),
-                (back_hbm, backward),
-                (gate_long_hbm, gate_long),
-            ]
+            [(long_filter_hbm, long_filter), (forward_hbm, forward), (back_hbm, backward)]
         )
     ]
     for load in loads:
         load.start()
 
-    def part(q):
-        return pl.ds(pl.multiple_of(q * chunk, chunk), chunk)
+    def own(q):
+        return pltpu.make_async_copy(
+            long_out.at[me, part(q), :], returned.at[me, part(q), :], own_sem.at[q]
+        )
 
     def rim(which, q):
         src, dst = ((mixed, halo_mixed), (first, halo_first))[which]
@@ -444,7 +459,10 @@
         halo_mixed[...] = jnp.zeros_like(halo_mixed)
         halo_first[...] = jnp.zeros_like(halo_first)
 
-    def early(q, _):
+    def early(q):
+        loaded(0, q).wait()
+        loaded(1, q).wait()
+
         def multiply(d, _):
             mixed[d, part(q), :] = (
                 key_ref[d, part(q), :].astype(jnp.float32)
@@ -457,6 +475,8 @@
         @pl.when(me < n - 1)
         def _():
             rim(0, q).start()
+
+        loaded(2, q).wait()
 
         def one(d, _):
             for j in range(groups):
@@ -482,12 +502,9 @@
         def _():
             rim(1, q).start()
 
-        return 0
-
-    lax.fori_loop(0, chunks, early, 0)
-    loads[0].wait()
-
-    def late(q, _):
+    def late(q):
+        loaded(3, q).wait()
+
         @pl.when(me > 0)
         def _():
             rim(0, q).wait_recv()
@@ -518,9 +535,16 @@
                     )
             if k:
                 there(k, q).start()
+
+    early(0)
+
+    def both(q, _):
+        early(q + 1)
+        late(q)
         return 0
 
-    lax.fori_loop(0, chunks, late, 0)
+    lax.fori_loop(0, chunks - 1, both, 0)
+    late(chunks - 1)
 
     def spread(values, at):
         bins = padded_bins(values)
@@ -529,8 +553,8 @@
             im = jnp.zeros_like(re) if im is None else im
             bins_in[r, at, :] = jnp.concatenate([re, im], axis=1).astype(jnp.bfloat16)
 
+    loads[0].wait()
     loads[1].wait()
-    loads[2].wait()
 
     def filter_rows(j, _):
         at = pl.ds(pl.multiple_of(j * ROWS, ROWS), ROWS)
@@ -544,7 +568,7 @@
         return 0
 
     lax.fori_loop(0, bin_count, filter_bin, 0)
-    loads[3].wait()
+    loads[2].wait()
 
     def convolve(q, _):
         for k in range(1, n):
@@ -590,33 +614,21 @@
         lax.fori_loop(0, groups, rows_out, 0)
         for k in range(1, n):
             home(k, q).start()
-        returned[me, part(q), :] = long_out[me, part(q), :]
+        own(q).start()
         return 0
 
     lax.fori_loop(0, chunks, convolve, 0)
-    loads[4].wait()
-
-    def finish(q, _):
-        for k in range(n):
-            if k:
-                home(k, q, True).wait_recv()
-            p = lax.rem(me + (n - k), n)
-            out_ref[p, part(q), :] = gated(
-                gate_long[p, part(q), :], returned[p, part(q), :].astype(jnp.float32)
-            )
-        return 0
-
-    lax.fori_loop(0, chunks, finish, 0)
-
     def drain(q, _):
         @pl.when(me < n - 1)
         def _():
             rim(0, q).wait_send()
             rim(1, q).wait_send()
 
+        own(q).wait()
         for k in range(1, n):
             there(k, q).wait_send()
             home(k, q).wait_send()
+            home(k, q, True).wait_recv()
         return 0
 
     lax.fori_loop(0, chunks, drain, 0)
@@ -673,13 +685,16 @@
     bf16, f32 = jnp.bfloat16, jnp.float32
     vmem = pl.BlockSpec(memory_space=pltpu.VMEM)
     anywhere = pl.BlockSpec(memory_space=pl.ANY)
+    in_hbm = pl.BlockSpec(memory_space=pltpu.HBM)
     dma = pltpu.SemaphoreType.DMA
     out = pl.pallas_call(
         functools.partial(whole_kernel, n, chunk),
         out_shape=jax.ShapeDtypeStruct((n, per, length), bf16),
-        in_specs=[vmem] * 6 + [anywhere] * 5,
-        out_specs=vmem,
+        in_specs=[vmem] * 3 + [in_hbm] * 7,
+        out_specs=anywhere,
         scratch_shapes=[
+            pltpu.VMEM((n, per, length), bf16),
+            pltpu.VMEM((n, per, length), bf16),
             pltpu.VMEM((n, per, length), bf16),
             pltpu.VMEM((n, per, length), bf16),
             pltpu.VMEM((per, total), bf16),
@@ -696,12 +711,13 @@
             pltpu.VMEM((n, per, length), bf16),
             pltpu.VMEM((n, per, length), bf16),
             pltpu.VMEM((n, per, length), bf16),
-            pltpu.VMEM((n, per, length), bf16),
             pltpu.VMEM((per, LANES), f32),
             pltpu.VMEM((bin_count, per, 2 * LANES), bf16),
             pltpu.VMEM((bin_count, per, 2 * LANES), f32),
             pltpu.VMEM((bin_count, chunk, 2 * LANES), f32),
-            dma((5,)),
+            dma((3,)),
+            dma((4, chunks)),
+            dma((chunks,)),
             dma((2, chunks)),
             dma((2, chunks)),
             dma((n, chunks)),
@@ -718,19 +734,18 @@
             transcendentals=0,
         ),
     )(
+        filter_first,
+        filter_second,
+        skip_gain.reshape(channels // LANES, LANES),
         cut(value_in),
         cut(key_in),
         cut(gate_first),
-        filter_first,
-        filter_second,
-        skip_gain.reshape(channels // LANES, LANES),
         cut(gate_second),
-        cut(gate_long),
         long_filter,
         jnp.asarray(forward),
         jnp.asarray(back),
     )
-    return out.reshape(channels, length)
+    return gated(gate_long, out.reshape(channels, length).astype(f32))
 
 
 def solution(mesh):

time: 37.7 us -> 38.8 us (1.029)
  other arithmetic: 0 us -> 2.48 us
  local copies, waits for them, and re-layouts: 2.26 us -> 0.01 us
  Pallas kernels: 35.3 us -> 36.1 us
    convert_element_type x0 -> x1, other arithmetic: none -> 2.48 us  [gated(): return (gate.astype(jnp.float32) * value).astype(jnp.bfloat16)]
    unnamed x1 -> x2, local copies, waits for them, and re-layouts: 2.26 us -> 0.01 us
    pallas_call x1, Pallas kernels: 35.3 us -> 36.1 us  [shards(): pl.pallas_call(functools.partial(whole_kernel, n, chunk), out_shape=jax.S...]
where the time goes in v1:
time: 38.8 us; the launch traced here: 38.6 us
  Pallas kernels  36.1 us (93%)
  other arithmetic  2.48 us (6%)
    pallas_call x1, Pallas kernels, shards(): pl.pallas_call(functools.partial(whole_kernel, n, chunk), out_shape=jax.S...  36.1 us
    convert_element_type x1, other arithmetic, gated(): return (gate.astype(jnp.float32) * value).astype(jnp.bfloat16)  2.48 us

profile of v1, /device:TPU:1, one launch (start us, length us, event | category | flops | bytes accessed | tf_op | source)
XLA Modules:
  0.0 38.6 jit_solution(16465207867994981711)
XLA Ops:
  0.0 0.0 copy-start
  0.0 36.1 %shard_map.109 = bf16[4,256,512]{2,1,0:T(8,128)(2,1)} custom-call(bf16[64,128]{1,0:T(8,128)(2,1)} %filter_first_ref.1, bf16[64,128]{1,0:T(8,128)(2,1)} %filter_second_ref.1, f32[8,128]{1,0:T(8,128)} %bitcast.12, bf16[4,256,512]{2,1,0:T(8,128)(2,1)} %bitcast.8, bf16[4,256,512]{2,1,0:T(8,128)(2,1)} %bitcast.9, bf16[4,256,512]{2,1,0:T(8,128)(2,1)} %bitcast.10, ...), custom_call_target="tpu_custom_call" | custom-call | flops 4294967296 | bytes 8388608 | tf_op jit(solution)/shard_map/pallas_call | solution.py:690
  36.1 0.0 copy-done
  36.1 2.5 %fusion = bf16[1024,512]{1,0:T(8,128)(2,1)} fusion(bf16[1024,512]{1,0:T(8,128)(2,1)S(1)} %copy-done, bf16[4,256,512]{2,1,0:T(8,128)(2,1)} %shard_map.109), kind=kLoop, calls=%fused_computation.1 | loop fusion | flops 2097152 | bytes 3145728 | tf_op jit(solution)/shard_map/convert_element_type | solution.py:309
Async XLA Ops:
  0.0 36.1 %copy-start = (bf16[1024,512]{1,0:T(8,128)(2,1)S(1)}, bf16[1024,512]{1,0:T(8,128)(2,1)}, u32[]{:S(2)}) copy-start(bf16[1024,512]{1,0:T(8,128)(2,1)} %param.15) | copy-start | bytes 3145732

commit v2 on v1

--- a/solution.py
+++ b/solution.py
@@ -344,6 +344,7 @@
     skip_wide,
     bins_in,
     spectrum,
+    products,
     bins_out,
     load_sem,
     part_sem,
@@ -463,14 +464,11 @@
         loaded(0, q).wait()
         loaded(1, q).wait()
 
-        def multiply(d, _):
+        for d in range(n):
             mixed[d, part(q), :] = (
                 key_ref[d, part(q), :].astype(jnp.float32)
                 * value_ref[d, part(q), :].astype(jnp.float32)
             ).astype(jnp.bfloat16)
-            return 0
-
-        lax.fori_loop(0, n, multiply, 0)
 
         @pl.when(me < n - 1)
         def _():
@@ -478,7 +476,7 @@
 
         loaded(2, q).wait()
 
-        def one(d, _):
+        for d in range(n):
             for j in range(groups):
                 g = d * (per // ROWS) + q * groups + j
                 w = band(taps_first[pl.ds(g, 1), :])
@@ -494,9 +492,6 @@
                     first[d, rows, lanes(b)] = gated(
                         gate_first_ref[d, rows, lanes(b)], result[(b - 1) * ROWS : b * ROWS]
                     )
-            return 0
-
-        lax.fori_loop(0, n, one, 0)
 
         @pl.when(me < n - 1)
         def _():
@@ -509,6 +504,14 @@
         def _():
             rim(0, q).wait_recv()
             rim(1, q).wait_recv()
+
+        for d in range(n):
+            for j in range(groups):
+                g = d * (per // ROWS) + q * groups + j
+                rows = rows_at(q, j)
+                head = jnp.concatenate([halo_mixed[d, rows, :], mixed[d, rows, lanes(0)]], axis=1)
+                head = jnp.dot(head, band_first[g], preferred_element_type=jnp.float32)
+                first[d, rows, lanes(0)] = gated(gate_first_ref[d, rows, lanes(0)], head)
 
         for k in [*range(2, n), 1, 0]:
             d = lax.rem(me + k, n)
@@ -516,19 +519,15 @@
             for j in range(groups):
                 g = d * (per // ROWS) + q * groups + j
                 rows = rows_at(q, j)
-                head = jnp.concatenate([halo_mixed[d, rows, :], mixed[d, rows, lanes(0)]], axis=1)
-                head = jnp.dot(head, band_first[g], preferred_element_type=jnp.float32)
-                head = gated(gate_first_ref[d, rows, lanes(0)], head)
-                parts = [halo_first[d, rows, :], head]
-                parts += [first[d, rows, lanes(b)] for b in range(1, blocks)]
-                windows = jnp.concatenate(
-                    [
-                        jnp.concatenate([parts[b], parts[b + 1]], axis=1)
-                        for b in range(blocks)
-                    ],
-                    axis=0,
+                ahead = jnp.concatenate([halo_first[d, rows, :], first[d, rows, lanes(0)]], axis=1)
+                windows = [ahead] + [
+                    first[d, rows, b * LANES - LANES : (b + 1) * LANES] for b in range(1, blocks)
+                ]
+                result = jnp.dot(
+                    jnp.concatenate(windows, axis=0),
+                    band_second[g],
+                    preferred_element_type=jnp.float32,
                 )
-                result = jnp.dot(windows, band_second[g], preferred_element_type=jnp.float32)
                 for b in range(blocks):
                     target[d, rows, lanes(b)] = gated(
                         gate_second[d, rows, lanes(b)], result[b * ROWS : (b + 1) * ROWS]
@@ -563,18 +562,19 @@
 
     lax.fori_loop(0, per // ROWS, filter_rows, 0)
 
-    def filter_bin(r, _):
+    for r in range(bin_count):
         spectrum[r] = jnp.dot(bins_in[r], forward[r], preferred_element_type=jnp.float32)
-        return 0
-
-    lax.fori_loop(0, bin_count, filter_bin, 0)
     loads[2].wait()
 
-    def convolve(q, _):
-        for k in range(1, n):
-            there(k, q, True).wait_recv()
-
-        def signal(j, rows):
+    span = bins_out.shape[1]
+    pieces = span // chunk
+
+    def convolve(w, _):
+        for c in range(pieces):
+            for k in range(1, n):
+                there(k, w * pieces + c, True).wait_recv()
+
+        def signal(rows):
             return [
                 gathered[a // blocks, rows, lanes(a % blocks)].astype(jnp.float32)
                 for a in range(total_blocks)
@@ -582,42 +582,49 @@
 
         def rows_in(j, _):
             at = pl.ds(pl.multiple_of(j * ROWS, ROWS), ROWS)
-            spread(signal(j, rows_at(q, j)), at)
+            spread(signal(rows_at(w * pieces, j)), at)
             return 0
 
-        lax.fori_loop(0, groups, rows_in, 0)
+        lax.fori_loop(0, span // ROWS, rows_in, 0)
+        here = pl.ds(pl.multiple_of(w * span, span), span)
 
         for r in range(bin_count):
-            sig = jnp.dot(bins_in[r, 0:chunk, :], forward[r], preferred_element_type=jnp.float32)
-            filt = spectrum[r, part(q), :]
+            sig = jnp.dot(bins_in[r, 0:span, :], forward[r], preferred_element_type=jnp.float32)
+            filt = spectrum[r, here, :]
             sig_re, sig_im = sig[:, :LANES], sig[:, LANES:]
             filt_re, filt_im = filt[:, :LANES], filt[:, LANES:]
-            product = jnp.concatenate(
+            products[r] = jnp.concatenate(
                 [sig_re * filt_re - sig_im * filt_im, sig_re * filt_im + sig_im * filt_re], axis=1
             ).astype(jnp.bfloat16)
-            bins_out[r] = jnp.dot(product, backward[r], preferred_element_type=jnp.float32)
-
-        def rows_out(j, _):
-            at = pl.ds(pl.multiple_of(j * ROWS, ROWS), ROWS)
-            rows = rows_at(q, j)
-            bins = {
-                r: (bins_out[r, at, :LANES], bins_out[r, at, LANES:]) for r in range(bin_count)
-            }
-            result = padded_back(bins, total_blocks)
-            skip = skip_wide[rows, :]
-            for a, value in enumerate(signal(j, rows)):
-                long_out[a // blocks, rows, lanes(a % blocks)] = (
-                    skip * value + result[a]
-                ).astype(jnp.bfloat16)
-            return 0
-
-        lax.fori_loop(0, groups, rows_out, 0)
-        for k in range(1, n):
-            home(k, q).start()
-        own(q).start()
+
+        for r in range(bin_count):
+            bins_out[r] = jnp.dot(products[r], backward[r], preferred_element_type=jnp.float32)
+
+        for c in range(pieces):
+            q = w * pieces + c
+
+            def rows_out(j, _):
+                at = pl.ds(pl.multiple_of(c * chunk + j * ROWS, ROWS), ROWS)
+                rows = rows_at(q, j)
+                bins = {
+                    r: (bins_out[r, at, :LANES], bins_out[r, at, LANES:]) for r in range(bin_count)
+                }
+                result = padded_back(bins, total_blocks)
+                skip = skip_wide[rows, :]
+                for a, value in enumerate(signal(rows)):
+                    long_out[a // blocks, rows, lanes(a % blocks)] = (
+                        skip * value + result[a]
+                    ).astype(jnp.bfloat16)
+                return 0
+
+            lax.fori_loop(0, groups, rows_out, 0)
+            for k in [*range(2, n), 1]:
+                home(k, q).start()
+            own(q).start()
         return 0
 
-    lax.fori_loop(0, chunks, convolve, 0)
+    lax.fori_loop(0, per // span, convolve, 0)
+
     def drain(q, _):
         @pl.when(me < n - 1)
         def _():
@@ -677,6 +684,7 @@
     per = channels // n
     total = n * length
     chunk = 64
+    span = 2 * chunk
     chunks = per // chunk
     group_count = filter_first.shape[0]
     bin_count = total // LANES + 1
@@ -714,7 +722,8 @@
             pltpu.VMEM((per, LANES), f32),
             pltpu.VMEM((bin_count, per, 2 * LANES), bf16),
             pltpu.VMEM((bin_count, per, 2 * LANES), f32),
-            pltpu.VMEM((bin_count, chunk, 2 * LANES), f32),
+            pltpu.VMEM((bin_count, span, 2 * LANES), bf16),
+            pltpu.VMEM((bin_count, span, 2 * LANES), f32),
             dma((3,)),
             dma((4, chunks)),
             dma((chunks,)),

time: 38.8 us -> 38.9 us (level)
  no operation moved by 1% of the time
where the time goes in v2:
time: 38.9 us; the launch traced here: 38.8 us
  Pallas kernels  36.3 us (93%)
  other arithmetic  2.48 us (6%)
    pallas_call x1, Pallas kernels, shards(): pl.pallas_call(functools.partial(whole_kernel, n, chunk), out_shape=jax.S...  36.3 us
    convert_element_type x1, other arithmetic, gated(): return (gate.astype(jnp.float32) * value).astype(jnp.bfloat16)  2.48 us

profile of v2, /device:TPU:1, one launch (start us, length us, event | category | flops | bytes accessed | tf_op | source)
XLA Modules:
  0.0 38.8 jit_solution(9687805267737748625)
XLA Ops:
  0.0 0.0 copy-start
  0.0 36.3 %shard_map.109 = bf16[4,256,512]{2,1,0:T(8,128)(2,1)} custom-call(bf16[64,128]{1,0:T(8,128)(2,1)} %filter_first_ref.1, bf16[64,128]{1,0:T(8,128)(2,1)} %filter_second_ref.1, f32[8,128]{1,0:T(8,128)} %bitcast.12, bf16[4,256,512]{2,1,0:T(8,128)(2,1)} %bitcast.8, bf16[4,256,512]{2,1,0:T(8,128)(2,1)} %bitcast.9, bf16[4,256,512]{2,1,0:T(8,128)(2,1)} %bitcast.10, ...), custom_call_target="tpu_custom_call" | custom-call | flops 4294967296 | bytes 8388608 | tf_op jit(solution)/shard_map/pallas_call | solution.py:698
  36.3 0.0 copy-done
  36.3 2.5 %fusion = bf16[1024,512]{1,0:T(8,128)(2,1)} fusion(bf16[1024,512]{1,0:T(8,128)(2,1)S(1)} %copy-done, bf16[4,256,512]{2,1,0:T(8,128)(2,1)} %shard_map.109), kind=kLoop, calls=%fused_computation.1 | loop fusion | flops 2097152 | bytes 3145728 | tf_op jit(solution)/shard_map/convert_element_type | solution.py:309
Async XLA Ops:
  0.0 36.3 %copy-start = (bf16[1024,512]{1,0:T(8,128)(2,1)S(1)}, bf16[1024,512]{1,0:T(8,128)(2,1)}, u32[]{:S(2)}) copy-start(bf16[1024,512]{1,0:T(8,128)(2,1)} %param.15) | copy-start | bytes 3145732

commit v3 on v2

--- a/solution.py
+++ b/solution.py
@@ -413,14 +413,15 @@
             device_id_type=MESH,
         )
 
-    def there(k, q, arriving=False):
+    def there(half, k, q, arriving=False):
         peer = lax.rem(me + (n - k if arriving else k), n)
         slot = peer if arriving else me
+        columns = slice(0, 2 * LANES) if half else slice(2 * LANES, length)
         return pltpu.make_async_remote_copy(
-            src_ref=second.at[peer, part(q), :],
-            dst_ref=gathered.at[slot, part(q), :],
-            send_sem=there_send.at[k, q],
-            recv_sem=there_recv.at[k, q],
+            src_ref=second.at[peer, part(q), columns],
+            dst_ref=gathered.at[slot, part(q), columns],
+            send_sem=there_send.at[half, k, q],
+            recv_sem=there_recv.at[half, k, q],
             device_id={"ctx": peer},
             device_id_type=MESH,
         )
@@ -481,25 +482,68 @@
                 g = d * (per // ROWS) + q * groups + j
                 w = band(taps_first[pl.ds(g, 1), :])
                 band_first[g] = w
-                band_second[g] = band(taps_second[pl.ds(g, 1), :])
                 rows = rows_at(q, j)
-                windows = jnp.concatenate(
-                    [mixed[d, rows, b * LANES - LANES : (b + 1) * LANES] for b in range(1, blocks)],
-                    axis=0,
+                result = jnp.dot(
+                    mixed[d, rows, length - 2 * LANES : length],
+                    w,
+                    preferred_element_type=jnp.float32,
                 )
-                result = jnp.dot(windows, w, preferred_element_type=jnp.float32)
-                for b in range(1, blocks):
-                    first[d, rows, lanes(b)] = gated(
-                        gate_first_ref[d, rows, lanes(b)], result[(b - 1) * ROWS : b * ROWS]
-                    )
+                first[d, rows, last] = gated(gate_first_ref[d, rows, last], result)
 
         @pl.when(me < n - 1)
         def _():
             rim(1, q).start()
 
-    def late(q):
+    def first_blocks(q, targets):
+        for d in range(n):
+            for j in range(groups):
+                rows = rows_at(q, j)
+                windows = [mixed[d, rows, b * LANES - LANES : (b + 1) * LANES] for b in targets]
+                result = jnp.dot(
+                    jnp.concatenate(windows, axis=0),
+                    band_first[d * (per // ROWS) + q * groups + j],
+                    preferred_element_type=jnp.float32,
+                )
+                for i, b in enumerate(targets):
+                    first[d, rows, lanes(b)] = gated(
+                        gate_first_ref[d, rows, lanes(b)], result[i * ROWS : (i + 1) * ROWS]
+                    )
+
+    def second_blocks(q, half, targets):
+        for k in [*range(2, n), 1, 0]:
+            d = lax.rem(me + k, n)
+            target = second if k else gathered
+            for j in range(groups):
+                g = d * (per // ROWS) + q * groups + j
+                rows = rows_at(q, j)
+                if half == 0:
+                    w = band(taps_second[pl.ds(g, 1), :])
+                    band_second[g] = w
+                else:
+                    w = band_second[g]
+                windows = [
+                    jnp.concatenate([halo_first[d, rows, :], first[d, rows, lanes(0)]], axis=1)
+                    if b == 0
+                    else first[d, rows, b * LANES - LANES : (b + 1) * LANES]
+                    for b in targets
+                ]
+                result = jnp.dot(
+                    jnp.concatenate(windows, axis=0), w, preferred_element_type=jnp.float32
+                )
+                for i, b in enumerate(targets):
+                    target[d, rows, lanes(b)] = gated(
+                        gate_second[d, rows, lanes(b)], result[i * ROWS : (i + 1) * ROWS]
+                    )
+            if k:
+                there(half, k, q).start()
+
+    def middle(q, _):
+        first_blocks(q, range(1, blocks - 1))
         loaded(3, q).wait()
-
+        second_blocks(q, 0, range(2, blocks))
+        return 0
+
+    def late(q, _):
         @pl.when(me > 0)
         def _():
             rim(0, q).wait_recv()
@@ -513,37 +557,16 @@
                 head = jnp.dot(head, band_first[g], preferred_element_type=jnp.float32)
                 first[d, rows, lanes(0)] = gated(gate_first_ref[d, rows, lanes(0)], head)
 
-        for k in [*range(2, n), 1, 0]:
-            d = lax.rem(me + k, n)
-            target = second if k else gathered
-            for j in range(groups):
-                g = d * (per // ROWS) + q * groups + j
-                rows = rows_at(q, j)
-                ahead = jnp.concatenate([halo_first[d, rows, :], first[d, rows, lanes(0)]], axis=1)
-                windows = [ahead] + [
-                    first[d, rows, b * LANES - LANES : (b + 1) * LANES] for b in range(1, blocks)
-                ]
-                result = jnp.dot(
-                    jnp.concatenate(windows, axis=0),
-                    band_second[g],
-                    preferred_element_type=jnp.float32,
-                )
-                for b in range(blocks):
-                    target[d, rows, lanes(b)] = gated(
-                        gate_second[d, rows, lanes(b)], result[b * ROWS : (b + 1) * ROWS]
-                    )
-            if k:
-                there(k, q).start()
-
-    early(0)
-
-    def both(q, _):
-        early(q + 1)
-        late(q)
+        second_blocks(q, 1, range(2))
         return 0
 
-    lax.fori_loop(0, chunks - 1, both, 0)
-    late(chunks - 1)
+    def start(q, _):
+        early(q)
+        return 0
+
+    lax.fori_loop(0, chunks, start, 0)
+    lax.fori_loop(0, chunks, middle, 0)
+    lax.fori_loop(0, chunks, late, 0)
 
     def spread(values, at):
         bins = padded_bins(values)
@@ -572,7 +595,8 @@
     def convolve(w, _):
         for c in range(pieces):
             for k in range(1, n):
-                there(k, w * pieces + c, True).wait_recv()
+                there(0, k, w * pieces + c, True).wait_recv()
+                there(1, k, w * pieces + c, True).wait_recv()
 
         def signal(rows):
             return [
@@ -633,12 +657,17 @@
 
         own(q).wait()
         for k in range(1, n):
-            there(k, q).wait_send()
+            there(0, k, q).wait_send()
+            there(1, k, q).wait_send()
             home(k, q).wait_send()
             home(k, q, True).wait_recv()
         return 0
 
     lax.fori_loop(0, chunks, drain, 0)
+
+
+def gate_kernel(gate_ref, value_ref, out_ref):
+    out_ref[...] = gated(gate_ref[...], value_ref[...].astype(jnp.float32))
 
 
 def fits_kernel(channels, length, n, tap_count):
@@ -647,7 +676,7 @@
     return (
         tap_count == LANES
         and length % LANES == 0
-        and length >= 2 * LANES
+        and length >= 3 * LANES
         and per % LANES == 0
         and n > 1
         and total & (total - 1) == 0
@@ -729,8 +758,8 @@
             dma((chunks,)),
             dma((2, chunks)),
             dma((2, chunks)),
-            dma((n, chunks)),
-            dma((n, chunks)),
+            dma((2, n, chunks)),
+            dma((2, n, chunks)),
             dma((n, chunks)),
             dma((n, chunks)),
         ],
@@ -754,7 +783,14 @@
         jnp.asarray(forward),
         jnp.asarray(back),
     )
-    return gated(gate_long, out.reshape(channels, length).astype(f32))
+    block = pl.BlockSpec((per, length), lambda i: (i, 0))
+    return pl.pallas_call(
+        gate_kernel,
+        out_shape=jax.ShapeDtypeStruct((channels, length), bf16),
+        grid=(n,),
+        in_specs=[block, block],
+        out_specs=block,
+    )(gate_long, out.reshape(channels, length))
 
 
 def solution(mesh):

time: 38.9 us -> 40.6 us (1.044)
  Pallas kernels: 36.3 us -> 40.4 us
  other arithmetic: 2.48 us -> 0 us
    pallas_call x0 -> x1, Pallas kernels: none -> 3.63 us  [shards(): pl.pallas_call(gate_kernel, out_shape=jax.ShapeDtypeStruct((channels, len...]
    convert_element_type x1 -> x0, other arithmetic: 2.48 us -> none  [gated(): return (gate.astype(jnp.float32) * value).astype(jnp.bfloat16)]
    pallas_call x1, Pallas kernels: 36.3 us -> 36.7 us  [shards(): pl.pallas_call(functools.partial(whole_kernel, n, chunk), out_shape=jax.S...]
where the time goes in v3:
time: 40.6 us; the launch traced here: 40.4 us
  Pallas kernels  40.4 us (100%)
    pallas_call x1, Pallas kernels, shards(): pl.pallas_call(functools.partial(whole_kernel, n, chunk), out_shape=jax.S...  36.7 us
    pallas_call x1, Pallas kernels, shards(): pl.pallas_call(gate_kernel, out_shape=jax.ShapeDtypeStruct((channels, len...  3.63 us

profile of v3, /device:TPU:1, one launch (start us, length us, event | category | flops | bytes accessed | tf_op | source)
XLA Modules:
  0.0 40.4 jit_solution(9297478982255692729)
XLA Ops:
  0.0 36.7 %shard_map.109 = bf16[4,256,512]{2,1,0:T(8,128)(2,1)} custom-call(bf16[64,128]{1,0:T(8,128)(2,1)} %filter_first_ref.1, bf16[64,128]{1,0:T(8,128)(2,1)} %filter_second_ref.1, f32[8,128]{1,0:T(8,128)} %bitcast.11, bf16[4,256,512]{2,1,0:T(8,128)(2,1)} %bitcast.7, bf16[4,256,512]{2,1,0:T(8,128)(2,1)} %bitcast.8, bf16[4,256,512]{2,1,0:T(8,128)(2,1)} %bitcast.9, ...), custom_call_target="tpu_custom_call" | custom-call | flops 4294967296 | bytes 8388608 | tf_op jit(solution)/shard_map/pallas_call | solution.py:727
  36.7 3.6 %shard_map.110 = bf16[1024,512]{1,0:T(8,128)(2,1)} custom-call(bf16[1024,512]{1,0:T(8,128)(2,1)} %gate_ref.1, bf16[1024,512]{1,0:T(8,128)(2,1)} %bitcast.6), custom_call_target="tpu_custom_call" | custom-call | tf_op jit(solution)/shard_map/pallas_call | solution.py:787

commit v4 on v2

--- a/solution.py
+++ b/solution.py
@@ -535,15 +535,16 @@
             if k:
                 there(k, q).start()
 
-    early(0)
-
-    def both(q, _):
-        early(q + 1)
+    def start(q, _):
+        early(q)
+        return 0
+
+    def follow(q, _):
         late(q)
         return 0
 
-    lax.fori_loop(0, chunks - 1, both, 0)
-    late(chunks - 1)
+    lax.fori_loop(0, chunks, start, 0)
+    lax.fori_loop(0, chunks, follow, 0)
 
     def spread(values, at):
         bins = padded_bins(values)
@@ -735,7 +736,7 @@
             dma((n, chunks)),
         ],
         compiler_params=pltpu.CompilerParams(
-            collective_id=0, has_side_effects=True, vmem_limit_bytes=56 * 1024 * 1024
+            collective_id=0, has_side_effects=True, vmem_limit_bytes=52 * 1024 * 1024
         ),
         cost_estimate=pl.CostEstimate(
             flops=8 * channels * length * 2 * LANES + 6 * 2 * per * total * 2 * LANES * 2,

time: 38.9 us -> 36.1 us (0.928)
  Pallas kernels: 36.3 us -> 32.2 us
  local copies, waits for them, and re-layouts: 0.01 us -> 2.12 us
  other arithmetic: 2.48 us -> 1.34 us
    pallas_call x1, Pallas kernels: 36.3 us -> 32.2 us  [shards(): pl.pallas_call(functools.partial(whole_kernel, n, chunk), out_shape=jax.S...]
    unnamed x2 -> x8, local copies, waits for them, and re-layouts: 0.01 us -> 2.12 us
    convert_element_type x1, other arithmetic: 2.48 us -> 1.34 us  [gated(): return (gate.astype(jnp.float32) * value).astype(jnp.bfloat16)]
where the time goes in v4:
time: 36.1 us; the launch traced here: 35.7 us
  Pallas kernels  32.2 us (89%)
  local copies, waits for them, and re-layouts  2.12 us (6%)
  other arithmetic  1.34 us (4%)
    pallas_call x1, Pallas kernels, shards(): pl.pallas_call(functools.partial(whole_kernel, n, chunk), out_shape=jax.S...  32.2 us
    unnamed x8, local copies, waits for them, and re-layouts  2.12 us
    convert_element_type x1, other arithmetic, gated(): return (gate.astype(jnp.float32) * value).astype(jnp.bfloat16)  1.34 us

profile of v4, /device:TPU:1, one launch (start us, length us, event | category | flops | bytes accessed | tf_op | source)
XLA Modules:
  0.0 35.7 jit_solution(5778976911469872711)
XLA Ops:
  0.0 0.0 copy-start
  0.0 0.7 %copy-done = bf16[64,128]{1,0:T(8,128)(2,1)S(1)} copy-done((bf16[64,128]{1,0:T(8,128)(2,1)S(1)}, bf16[64,128]{1,0:T(8,128)(2,1)}, u32[]{:S(2)}) %copy-start) | copy-done | bytes 16408
  0.7 0.0 copy-start.1
  0.7 0.7 %copy-done.1 = bf16[64,128]{1,0:T(8,128)(2,1)S(1)} copy-done((bf16[64,128]{1,0:T(8,128)(2,1)S(1)}, bf16[64,128]{1,0:T(8,128)(2,1)}, u32[]{:S(2)}) %copy-start.1) | copy-done | bytes 16408
  1.4 0.0 copy-start.2
  1.4 0.7 %copy-done.2 = f32[1024]{0:T(1024)S(1)} copy-done((f32[1024]{0:T(1024)S(1)}, f32[1024]{0:T(1024)}, u32[]{:S(2)}) %copy-start.2) | copy-done | bytes 4120
  2.1 0.0 copy-start.3
  2.1 32.2 %shard_map.109 = bf16[4,256,512]{2,1,0:T(8,128)(2,1)S(1)} custom-call(bf16[64,128]{1,0:T(8,128)(2,1)S(1)} %copy-done, bf16[64,128]{1,0:T(8,128)(2,1)S(1)} %copy-done.1, f32[8,128]{1,0:T(8,128)S(1)} %bitcast.8, bf16[4,256,512]{2,1,0:T(8,128)(2,1)} %bitcast.9, bf16[4,256,512]{2,1,0:T(8,128)(2,1)} %bitcast.10, bf16[4,256,512]{2,1,0:T(8,128)(2,1)} %bitcast.11, ...), custom_call_target="tpu_custom_call" | custom-call | flops 4294967296 | bytes 8388608 | tf_op jit(solution)/shard_map/pallas_call | solution.py:699
  34.4 0.0 copy-done.3
  34.4 1.3 %fusion = bf16[1024,512]{1,0:T(8,128)(2,1)} fusion(bf16[1024,512]{1,0:T(8,128)(2,1)S(1)} %copy-done.3, bf16[4,256,512]{2,1,0:T(8,128)(2,1)S(1)} %shard_map.109), kind=kLoop, calls=%fused_computation.1 | loop fusion | flops 2097152 | bytes 3145728 | tf_op jit(solution)/shard_map/convert_element_type | solution.py:309
Async XLA Ops:
  0.0 0.7 %copy-start = (bf16[64,128]{1,0:T(8,128)(2,1)S(1)}, bf16[64,128]{1,0:T(8,128)(2,1)}, u32[]{:S(2)}) copy-start(bf16[64,128]{1,0:T(8,128)(2,1)} %filter_first_ref.1) | copy-start | bytes 49156
  0.7 0.7 %copy-start.1 = (bf16[64,128]{1,0:T(8,128)(2,1)S(1)}, bf16[64,128]{1,0:T(8,128)(2,1)}, u32[]{:S(2)}) copy-start(bf16[64,128]{1,0:T(8,128)(2,1)} %filter_second_ref.1) | copy-start | bytes 49156
  1.4 0.7 %copy-start.2 = (f32[1024]{0:T(1024)S(1)}, f32[1024]{0:T(1024)}, u32[]{:S(2)}) copy-start(f32[1024]{0:T(1024)} %param.19) | copy-start | bytes 12292
  2.1 32.2 %copy-start.3 = (bf16[1024,512]{1,0:T(8,128)(2,1)S(1)}, bf16[1024,512]{1,0:T(8,128)(2,1)}, u32[]{:S(2)}) copy-start(bf16[1024,512]{1,0:T(8,128)(2,1)} %param.15) | copy-start | bytes 3145732

commit v5 on v4

--- a/solution.py
+++ b/solution.py
@@ -744,16 +744,21 @@
             transcendentals=0,
         ),
     )(
-        filter_first,
-        filter_second,
-        skip_gain.reshape(channels // LANES, LANES),
-        cut(value_in),
-        cut(key_in),
-        cut(gate_first),
-        cut(gate_second),
-        long_filter,
-        jnp.asarray(forward),
-        jnp.asarray(back),
+        *[
+            pltpu.with_memory_space_constraint(a, pltpu.HBM)
+            for a in (
+                filter_first,
+                filter_second,
+                skip_gain.reshape(channels // LANES, LANES),
+                cut(value_in),
+                cut(key_in),
+                cut(gate_first),
+                cut(gate_second),
+                long_filter,
+                jnp.asarray(forward),
+                jnp.asarray(back),
+            )
+        ]
     )
     return gated(gate_long, out.reshape(channels, length).astype(f32))
 

time: 36.1 us -> 34.6 us (0.958)
  local copies, waits for them, and re-layouts: 2.12 us -> 0.01 us
  Pallas kernels: 32.2 us -> 33.1 us
    unnamed x8 -> x2, local copies, waits for them, and re-layouts: 2.12 us -> 0.01 us
    pallas_call x1, Pallas kernels: 32.2 us -> 33.1 us  [shards(): pl.pallas_call(functools.partial(whole_kernel, n, chunk), out_shape=jax.S...]
where the time goes in v5:
time: 34.6 us; the launch traced here: 34.4 us
  Pallas kernels  33.1 us (96%)
  other arithmetic  1.32 us (4%)
    pallas_call x1, Pallas kernels, shards(): pl.pallas_call(functools.partial(whole_kernel, n, chunk), out_shape=jax.S...  33.1 us
    convert_element_type x1, other arithmetic, gated(): return (gate.astype(jnp.float32) * value).astype(jnp.bfloat16)  1.32 us

profile of v5, /device:TPU:1, one launch (start us, length us, event | category | flops | bytes accessed | tf_op | source)
XLA Modules:
  0.0 34.4 jit_solution(16119716313553561791)
XLA Ops:
  0.0 0.0 copy-start
  0.0 33.1 %shard_map.109 = bf16[4,256,512]{2,1,0:T(8,128)(2,1)S(1)} custom-call(bf16[64,128]{1,0:T(8,128)(2,1)} %filter_first_ref.1, bf16[64,128]{1,0:T(8,128)(2,1)} %filter_second_ref.1, f32[8,128]{1,0:T(8,128)} %bitcast.12, bf16[4,256,512]{2,1,0:T(8,128)(2,1)} %bitcast.8, bf16[4,256,512]{2,1,0:T(8,128)(2,1)} %bitcast.9, bf16[4,256,512]{2,1,0:T(8,128)(2,1)} %bitcast.10, ...), custom_call_target="tpu_custom_call" | custom-call | flops 4294967296 | bytes 8388608 | tf_op jit(solution)/shard_map/pallas_call | solution.py:699
  33.1 0.0 copy-done
  33.1 1.3 %fusion = bf16[1024,512]{1,0:T(8,128)(2,1)} fusion(bf16[1024,512]{1,0:T(8,128)(2,1)S(1)} %copy-done, bf16[4,256,512]{2,1,0:T(8,128)(2,1)S(1)} %shard_map.109), kind=kLoop, calls=%fused_computation.1 | loop fusion | flops 2097152 | bytes 3145728 | tf_op jit(solution)/shard_map/convert_element_type | solution.py:309
Async XLA Ops:
  0.0 33.1 %copy-start = (bf16[1024,512]{1,0:T(8,128)(2,1)S(1)}, bf16[1024,512]{1,0:T(8,128)(2,1)}, u32[]{:S(2)}) copy-start(bf16[1024,512]{1,0:T(8,128)(2,1)} %param.15) | copy-start | bytes 3145732

commit v6 on v5

--- a/solution.py
+++ b/solution.py
@@ -685,7 +685,7 @@
     per = channels // n
     total = n * length
     chunk = 64
-    span = 2 * chunk
+    span = chunk
     chunks = per // chunk
     group_count = filter_first.shape[0]
     bin_count = total // LANES + 1

time: 34.6 us -> 34.6 us (level)
  no operation moved by 1% of the time
where the time goes in v6:
time: 34.6 us; the launch traced here: 34.4 us
  Pallas kernels  33.1 us (96%)
  other arithmetic  1.32 us (4%)
    pallas_call x1, Pallas kernels, shards(): pl.pallas_call(functools.partial(whole_kernel, n, chunk), out_shape=jax.S...  33.1 us
    convert_element_type x1, other arithmetic, gated(): return (gate.astype(jnp.float32) * value).astype(jnp.bfloat16)  1.32 us

profile of v6, /device:TPU:1, one launch (start us, length us, event | category | flops | bytes accessed | tf_op | source)
XLA Modules:
  0.0 34.4 jit_solution(8747851932578126146)
XLA Ops:
  0.0 0.0 copy-start
  0.0 33.1 %shard_map.109 = bf16[4,256,512]{2,1,0:T(8,128)(2,1)S(1)} custom-call(bf16[64,128]{1,0:T(8,128)(2,1)} %filter_first_ref.1, bf16[64,128]{1,0:T(8,128)(2,1)} %filter_second_ref.1, f32[8,128]{1,0:T(8,128)} %bitcast.12, bf16[4,256,512]{2,1,0:T(8,128)(2,1)} %bitcast.8, bf16[4,256,512]{2,1,0:T(8,128)(2,1)} %bitcast.9, bf16[4,256,512]{2,1,0:T(8,128)(2,1)} %bitcast.10, ...), custom_call_target="tpu_custom_call" | custom-call | flops 4294967296 | bytes 8388608 | tf_op jit(solution)/shard_map/pallas_call | solution.py:699
  33.1 0.0 copy-done
  33.1 1.3 %fusion = bf16[1024,512]{1,0:T(8,128)(2,1)} fusion(bf16[1024,512]{1,0:T(8,128)(2,1)S(1)} %copy-done, bf16[4,256,512]{2,1,0:T(8,128)(2,1)S(1)} %shard_map.109), kind=kLoop, calls=%fused_computation.1 | loop fusion | flops 2097152 | bytes 3145728 | tf_op jit(solution)/shard_map/convert_element_type | solution.py:309
Async XLA Ops:
  0.0 33.1 %copy-start = (bf16[1024,512]{1,0:T(8,128)(2,1)S(1)}, bf16[1024,512]{1,0:T(8,128)(2,1)}, u32[]{:S(2)}) copy-start(bf16[1024,512]{1,0:T(8,128)(2,1)} %param.15) | copy-start | bytes 3145732

commit v7 on v5

--- a/solution.py
+++ b/solution.py
@@ -684,7 +684,7 @@
         )
     per = channels // n
     total = n * length
-    chunk = 64
+    chunk = 32
     span = 2 * chunk
     chunks = per // chunk
     group_count = filter_first.shape[0]

time: 34.6 us -> 35.4 us (1.023)
  Pallas kernels: 33.1 us -> 33.9 us
    pallas_call x1, Pallas kernels: 33.1 us -> 33.9 us  [shards(): pl.pallas_call(functools.partial(whole_kernel, n, chunk), out_shape=jax.S...]
where the time goes in v7:
time: 35.4 us; the launch traced here: 35.3 us
  Pallas kernels  33.9 us (96%)
  other arithmetic  1.32 us (4%)
    pallas_call x1, Pallas kernels, shards(): pl.pallas_call(functools.partial(whole_kernel, n, chunk), out_shape=jax.S...  33.9 us
    convert_element_type x1, other arithmetic, gated(): return (gate.astype(jnp.float32) * value).astype(jnp.bfloat16)  1.32 us

profile of v7, /device:TPU:1, one launch (start us, length us, event | category | flops | bytes accessed | tf_op | source)
XLA Modules:
  0.0 35.3 jit_solution(9244898546442015679)
XLA Ops:
  0.0 0.0 copy-start
  0.0 33.9 %shard_map.109 = bf16[4,256,512]{2,1,0:T(8,128)(2,1)S(1)} custom-call(bf16[64,128]{1,0:T(8,128)(2,1)} %filter_first_ref.1, bf16[64,128]{1,0:T(8,128)(2,1)} %filter_second_ref.1, f32[8,128]{1,0:T(8,128)} %bitcast.12, bf16[4,256,512]{2,1,0:T(8,128)(2,1)} %bitcast.8, bf16[4,256,512]{2,1,0:T(8,128)(2,1)} %bitcast.9, bf16[4,256,512]{2,1,0:T(8,128)(2,1)} %bitcast.10, ...), custom_call_target="tpu_custom_call" | custom-call | flops 4294967296 | bytes 8388608 | tf_op jit(solution)/shard_map/pallas_call | solution.py:699
  33.9 0.0 copy-done
  33.9 1.3 %fusion = bf16[1024,512]{1,0:T(8,128)(2,1)} fusion(bf16[1024,512]{1,0:T(8,128)(2,1)S(1)} %copy-done, bf16[4,256,512]{2,1,0:T(8,128)(2,1)S(1)} %shard_map.109), kind=kLoop, calls=%fused_computation.1 | loop fusion | flops 2097152 | bytes 3145728 | tf_op jit(solution)/shard_map/convert_element_type | solution.py:309
Async XLA Ops:
  0.0 33.9 %copy-start = (bf16[1024,512]{1,0:T(8,128)(2,1)S(1)}, bf16[1024,512]{1,0:T(8,128)(2,1)}, u32[]{:S(2)}) copy-start(bf16[1024,512]{1,0:T(8,128)(2,1)} %param.15) | copy-start | bytes 3145732
